TPU v7x, 32 devices: a whole 2x2x4 slice. The times are simulated.
32 devices in a mesh: row: 8 (over z, y), col: 4 (over x, core).
Axes of the slice: x: 2, y: 2, z: 4, core: 2. Of those that a mesh axis runs over, the one named last changes fastest.
Arguments:
- object_field: float32 [2, 3072, 1024], P(None, 'row', 'col'), may hold values from -3 to 3
- probe_field: float32 [2, 256, 256], replicated, may hold values from -6 to 6
- amplitudes: bfloat16 [8, 4, 4, 256, 256], P('row', 'col'), may hold values from 0.5 to 16
- pos_rows: int32 [8, 4, 4], P('row', 'col'), may hold values from 0 to 383
- pos_cols: int32 [8, 4, 4], P('row', 'col'), may hold values from 0 to 255
- scan_pick: int32 [8, 4, 2], P('row', 'col'), may hold values from 0 to 3
- scan_count: int32 [32], P(('row', 'col')), may hold values from 1 to 2, 48 in all
Outputs:
- object_next: float32 [2, 3072, 1024], P(None, 'row', 'col')
- probe_next: float32 [2, 256, 256], replicated
Inputs may be any that keep to these rules, and one draw needn't show every extreme that they name: `scan_count`: each tile's list has 1 to 2 scans; the longest list has exactly 2; lists total 48 scans.
All inputs are finite; a program needn't handle non-finite values. No bound on the sum of `scan_count` on one device may be relied on, other than what follows from the above.
Results may differ from a plain program's by a relative error of at most 0.0003.
Values sent between devices are 32-bit elements; how exact they have to be, the bound alone decides.
A program may use at most 64 MiB of HBM per device.

v0:
```python
import functools
import math

import jax
import jax.numpy as jnp
import ml_dtypes
import numpy as np
from jax import lax
from jax.experimental import pallas as pl
from jax.experimental.pallas import tpu as pltpu
from jax.sharding import PartitionSpec as P

SOFTENING = 0.25
OBJECT_REG = 0.5
PROBE_REG = 1.0
MESH = pl.DeviceIdType.MESH
VMEM_BYTES = 48 * 1024 * 1024
SUB = 8
WAYS = [(-1, 0), (1, 0), (0, -1), (0, 1), (-1, -1), (-1, 1), (1, -1), (1, 1)]
F32 = jnp.float32


def place(mesh_shape):
    return (lax.axis_index("row"), lax.axis_index("col"))


def exists(at, way, sizes, sign):
    conds = []
    for pos, step, size in zip(at, way, sizes):
        if step * sign == 1:
            conds.append(pos < size - 1)
        elif step * sign == -1:
            conds.append(pos > 0)
    return functools.reduce(jnp.logical_and, conds)


def greet(barrier, at, sizes, extra):
    total = jnp.int32(len(extra))
    for way in WAYS:
        here = exists(at, way, sizes, 1)

        @pl.when(here)
        def _(way=way):
            pl.semaphore_signal(
                barrier, inc=1, device_id=(at[0] + way[0], at[1] + way[1]), device_id_type=MESH
            )

        total = total + here.astype(jnp.int32)
    for peer in extra:
        pl.semaphore_signal(barrier, inc=1, device_id=peer, device_id_type=MESH)
    pl.semaphore_wait(barrier, total)


def halo_kernel(sizes, rim, obj, ext, send_sem, recv_sem, own_sem):
    high, wide = obj.shape[1:]
    at = place(sizes)
    greet(pltpu.get_barrier_semaphore(), at, sizes, [])
    src = {-1: lambda n: (0, rim), 0: lambda n: (0, n), 1: lambda n: (n - rim, rim)}
    dst = {-1: lambda n: (rim + n, rim), 0: lambda n: (rim, n), 1: lambda n: (0, rim)}

    def cut(ref, table, way):
        r, c = table[way[0]](high), table[way[1]](wide)
        return ref.at[:, pl.ds(*r), pl.ds(*c)]

    copies = [
        pltpu.make_async_remote_copy(
            src_ref=cut(obj, src, way),
            dst_ref=cut(ext, dst, way),
            send_sem=send_sem.at[k],
            recv_sem=recv_sem.at[k],
            device_id=(at[0] + way[0], at[1] + way[1]),
            device_id_type=MESH,
        )
        for k, way in enumerate(WAYS)
    ]
    for copy, way in zip(copies, WAYS):
        pl.when(exists(at, way, sizes, 1))(copy.start)
    own = pltpu.make_async_copy(obj, ext.at[:, pl.ds(rim, high), pl.ds(rim, wide)], own_sem)
    own.start()
    for way in WAYS:

        @pl.when(jnp.logical_not(exists(at, way, sizes, -1)))
        def _(way=way):
            (r, nr), (c, nc) = dst[way[0]](high), dst[way[1]](wide)
            ext[:, r : r + nr, c : c + nc] = jnp.zeros((2, nr, nc), F32)

    own.wait()
    for copy, way in zip(copies, WAYS):
        pl.when(exists(at, way, sizes, 1))(copy.wait_send)
        pl.when(exists(at, way, sizes, -1))(copy.wait_recv)


def split(x):
    hi = x.astype(jnp.bfloat16)
    return hi, (x - hi.astype(F32)).astype(jnp.bfloat16)


def dot(a, b):
    return jnp.dot(a, b, preferred_element_type=F32)


def left(table_hi, table_lo, x):
    hi, lo = split(x)
    return dot(table_hi[...], hi) + (dot(table_hi[...], lo) + dot(table_lo[...], hi))


def right(x, table_hi, table_lo):
    hi, lo = split(x)
    return dot(hi, table_hi[...]) + (dot(lo, table_hi[...]) + dot(hi, table_lo[...]))


def work_kernel(
    rows, cols, picks, count, ext, probe, amps, m_hi, m_lo, n_hi, n_lo, grad, sums, obj, wave
):
    width = probe.shape[1]
    slots = picks.shape[0]
    span = ext.shape[2]
    for s in range(slots):
        r, c = rows[picks[s]], cols[picks[s]]
        for p in range(2):
            base = pl.multiple_of(r // SUB * SUB, SUB)
            tall = width + SUB
            band = pltpu.roll(ext[p, pl.ds(base, tall), :], lax.rem(span - c, span), 1)[:, :width]
            obj[s, p] = pltpu.roll(band, lax.rem(tall - r % SUB, tall), 0)[:width]
    pr, pi = probe[0], probe[1]
    for s in range(slots):
        here = slice(s * width, (s + 1) * width)
        wave[:width, here] = pr * obj[s, 0] - pi * obj[s, 1]
        wave[width:, here] = pr * obj[s, 1] + pi * obj[s, 0]

    def turn(x):
        return jnp.concatenate(
            [
                jnp.concatenate(
                    [x[:width, s * width : (s + 1) * width], x[width:, s * width : (s + 1) * width]],
                    axis=1,
                )
                for s in range(slots)
            ],
            axis=0,
        )

    far = right(turn(left(m_hi, m_lo, wave[...])), n_hi, n_lo)
    for s in range(slots):
        here = slice(s * width, (s + 1) * width)
        live = (count[0] > s).astype(F32)
        fr, fi = far[here, :width], far[here, width:]
        measured = amps[picks[s]].astype(F32)
        weight = (measured * lax.rsqrt(fr * fr + fi * fi + SOFTENING) - 1.0) * live
        wave[:width, here] = fr * weight
        wave[width:, here] = fi * weight
    back = right(turn(left(n_hi, n_lo, wave[...])), m_hi, m_lo)
    grad[...] = jnp.zeros(grad.shape, F32)
    lamp = pr * pr + pi * pi
    totals = [jnp.zeros((width, width), F32)] * 3
    for s in range(slots):
        here = slice(s * width, (s + 1) * width)
        live = (count[0] > s).astype(F32)
        br, bi = back[here, :width], back[here, width:]
        o_r, o_i = obj[s, 0], obj[s, 1]
        totals[0] = totals[0] + (o_r * br + o_i * bi)
        totals[1] = totals[1] + (o_r * bi - o_i * br)
        totals[2] = totals[2] + live * (o_r * o_r + o_i * o_i)
        r, c = rows[picks[s]], cols[picks[s]]
        pieces = (pr * br + pi * bi, pr * bi - pi * br, live * lamp)
        for p, piece in enumerate(pieces):
            base = pl.multiple_of(r // SUB * SUB, SUB)
            piece = jnp.concatenate([piece, jnp.zeros((SUB, width), F32)], axis=0)
            piece = pltpu.roll(piece, r % SUB, 0)
            piece = jnp.concatenate([piece, jnp.zeros((width + SUB, span - width), F32)], axis=1)
            grad[p, pl.ds(base, width + SUB), :] += pltpu.roll(piece, c, 1)
    for p in range(3):
        sums[p] = totals[p].reshape(width // SUB, SUB, width)


def stages(sizes):
    out = []
    for axis in (1, 0):
        stride, rest = 1, sizes[axis]
        while rest > 1:
            p = next(f for f in range(2, rest + 1) if rest % f == 0)
            out.append((axis, stride, p))
            stride, rest = stride * p, rest // p
    return out


def fold_kernel(sizes, rim, steps, n_in, *refs):
    grad, sums, obj, probe, obj_out, probe_out, acc, cen = refs[:8]
    bufs = refs[8 : 8 + len(WAYS)]
    stage_bufs = refs[8 + len(WAYS) : 8 + len(WAYS) + len(steps)]
    send_sem, recv_sem, rs_send, rs_recv, ag_send, ag_recv = refs[8 + len(WAYS) + len(steps) :]
    high, wide = obj.shape[1:]
    at = place(sizes)

    def peer(step, k):
        axis, stride, p, _, _ = step
        digit = lax.rem(at[axis] // stride, p)
        other = lax.rem(digit + k, p)
        index = at[axis] + (other - digit) * stride
        return ((index, at[1]) if axis == 0 else (at[0], index)), digit, other

    everyone = [peer(step, k)[0] for step in steps for k in range(1, step[2])]
    greet(pltpu.get_barrier_semaphore(), at, sizes, everyone)

    src = {-1: lambda n: (0, rim), 0: lambda n: (rim, n), 1: lambda n: (rim + n, rim)}
    dst = {-1: lambda n: (n - rim, rim), 0: lambda n: (0, n), 1: lambda n: (0, rim)}
    copies = []
    for k, way in enumerate(WAYS):
        r, c = src[way[0]](high), src[way[1]](wide)
        copies.append(
            pltpu.make_async_remote_copy(
                src_ref=grad.at[:, pl.ds(*r), pl.ds(*c)],
                dst_ref=bufs[k],
                send_sem=send_sem.at[k],
                recv_sem=recv_sem.at[k],
                device_id=(at[0] + way[0], at[1] + way[1]),
                device_id_type=MESH,
            )
        )

    def begin_halo():
        for copy, way in zip(copies, WAYS):
            pl.when(exists(at, way, sizes, 1))(copy.start)

    acc[...] = sums[...]
    units = sums.shape[1]
    off = jnp.int32(0)
    pending = []
    undo = []
    sem = 0
    for i, step in enumerate(steps):
        axis, stride, p, size, scatter = step
        part = size // p if scatter else size
        moved = []
        for k in range(1, p):
            device, digit, other = peer(step, k)
            start = off + other * part if scatter else off
            copy = pltpu.make_async_remote_copy(
                src_ref=acc.at[:, pl.ds(start, part)],
                dst_ref=stage_bufs[i].at[k],
                send_sem=rs_send.at[sem],
                recv_sem=rs_recv.at[sem],
                device_id=device,
                device_id_type=MESH,
            )
            copy.start()
            moved.append(copy)
            sem += 1
        if i == 0:
            begin_halo()
        digit = peer(step, 1)[1]
        for copy in moved:
            copy.wait_recv()
        if scatter:
            undo.append((step, off, part))
            off = off + digit * part
            pending += moved
            total = acc[:, pl.ds(off, part)]
            for k in range(1, p):
                total = total + stage_bufs[i][k]
            acc[:, pl.ds(off, part)] = total
        else:
            for copy in moved:
                copy.wait_send()
            stage_bufs[i][0] = acc[:, pl.ds(off, part)]
            total = jnp.zeros((3, part) + acc.shape[2:], F32)
            for j in range(p):
                total = total + stage_bufs[i][lax.rem(digit - j + p, p)]
            acc[:, pl.ds(off, part)] = total
    part = steps[-1][3] // steps[-1][2] if steps[-1][4] else steps[-1][3]
    reg = acc[2, pl.ds(off, part)] + PROBE_REG
    for p in range(2):
        probe_out[p, pl.ds(off, part)] = probe[p, pl.ds(off, part)] + acc[p, pl.ds(off, part)] / reg

    def finish_object():
        cen[...] = grad[:, rim : rim + high, rim : rim + wide]
        for k, (copy, way) in enumerate(zip(copies, WAYS)):

            @pl.when(exists(at, way, sizes, -1))
            def _(k=k, copy=copy, way=way):
                copy.wait_recv()
                (r, nr), (c, nc) = dst[way[0]](high), dst[way[1]](wide)
                cen[:, r : r + nr, c : c + nc] += bufs[k][...]

        light = cen[2] + OBJECT_REG
        for p in range(2):
            obj_out[p] = obj[p] + cen[p] / light

    sem = 0
    for n, (step, base, part) in enumerate(reversed(undo)):
        p = step[2]
        moved = []
        for k in range(1, p):
            device, digit, other = peer(step, k)
            here = probe_out.at[:, pl.ds(base + digit * part, part)]
            copy = pltpu.make_async_remote_copy(
                src_ref=here,
                dst_ref=here,
                send_sem=ag_send.at[sem],
                recv_sem=ag_recv.at[sem],
                device_id=device,
                device_id_type=MESH,
            )
            copy.start()
            moved.append(copy)
            sem += 1
        for copy in moved:
            copy.wait_recv()
        pending += moved
    finish_object()
    for copy in pending:
        copy.wait_send()
    for copy, way in zip(copies, WAYS):
        pl.when(exists(at, way, sizes, 1))(copy.wait_send)


def tables(width):
    grid = np.arange(width)
    angle = (grid[:, None] * grid[None, :] % width) * (2.0 * math.pi / width)
    cos, sin = np.cos(angle) / math.sqrt(width), -np.sin(angle) / math.sqrt(width)
    out = []
    for full in (np.block([[cos, -sin], [sin, cos]]), np.block([[cos, sin], [-sin, cos]])):
        full = full.astype(np.float32)
        hi = full.astype(ml_dtypes.bfloat16)
        out += [hi, (full - hi.astype(np.float32)).astype(ml_dtypes.bfloat16)]
    return out


def per_device(
    sizes, object_field, probe_field, amplitudes, pos_rows, pos_cols, scan_pick, scan_count
):
    _, high, wide = object_field.shape
    width = probe_field.shape[1]
    rim = width // 2
    slots = scan_pick.shape[2]
    vmem = pl.BlockSpec(memory_space=pltpu.VMEM)
    smem = pl.BlockSpec(memory_space=pltpu.SMEM)
    dma = pltpu.SemaphoreType.DMA
    outer = (high + 2 * rim, wide + 2 * rim)
    ext = pl.pallas_call(
        functools.partial(halo_kernel, sizes, rim),
        out_shape=jax.ShapeDtypeStruct((2,) + outer, F32),
        in_specs=[vmem],
        out_specs=vmem,
        scratch_shapes=[dma((len(WAYS),)), dma((len(WAYS),)), dma],
        compiler_params=pltpu.CompilerParams(
            collective_id=0, has_side_effects=True, vmem_limit_bytes=VMEM_BYTES
        ),
        name="object_halo",
    )(object_field)
    grad, sums = pl.pallas_call(
        work_kernel,
        out_shape=[
            jax.ShapeDtypeStruct((3,) + outer, F32),
            jax.ShapeDtypeStruct((3, width // SUB, SUB, width), F32),
        ],
        in_specs=[smem] * 4 + [vmem] * 7,
        out_specs=[vmem, vmem],
        scratch_shapes=[
            pltpu.VMEM((slots, 2, width, width), F32),
            pltpu.VMEM((2 * width, slots * width), F32),
        ],
        compiler_params=pltpu.CompilerParams(vmem_limit_bytes=VMEM_BYTES),
        name="scan_terms",
    )(
        pos_rows[0, 0],
        pos_cols[0, 0],
        scan_pick[0, 0],
        scan_count,
        ext,
        probe_field,
        amplitudes[0, 0],
        *tables(width),
    )
    size = width // SUB
    steps = []
    for axis, stride, p in stages(sizes):
        scatter = size % p == 0
        steps.append((axis, stride, p, size, scatter))
        size = size // p if scatter else size
    sems = sum(step[2] - 1 for step in steps)
    lengths = {-1: lambda n: rim, 0: lambda n: n, 1: lambda n: rim}
    object_next, probe_next = pl.pallas_call(
        functools.partial(fold_kernel, sizes, rim, steps, 4),
        out_shape=[
            jax.ShapeDtypeStruct(object_field.shape, F32),
            jax.ShapeDtypeStruct((2, width // SUB, SUB, width), F32),
        ],
        in_specs=[vmem] * 4,
        out_specs=[vmem, vmem],
        scratch_shapes=[
            pltpu.VMEM((3, width // SUB, SUB, width), F32),
            pltpu.VMEM((3, high, wide), F32),
        ]
        + [pltpu.VMEM((3, lengths[r](high), lengths[c](wide)), F32) for r, c in WAYS]
        + [
            pltpu.VMEM((p, 3, size // p if scatter else size, SUB, width), F32)
            for _, _, p, size, scatter in steps
        ]
        + [dma((len(WAYS),)), dma((len(WAYS),))]
        + [dma((sems,))] * 4,
        compiler_params=pltpu.CompilerParams(
            collective_id=1, has_side_effects=True, vmem_limit_bytes=VMEM_BYTES
        ),
        name="fold",
    )(grad, sums, object_field, probe_field.reshape(2, width // SUB, SUB, width))
    return object_next, probe_next.reshape(probe_field.shape)


def solution(mesh):
    sizes = (mesh.shape["row"], mesh.shape["col"])
    in_specs = (
        P(None, "row", "col"),
        P(),
        P("row", "col", None, None, None),
        P("row", "col", None),
        P("row", "col", None),
        P("row", "col", None),
        P(("row", "col")),
    )
    out_specs = (P(None, "row", "col"), P())
    return jax.shard_map(
        functools.partial(per_device, sizes),
        mesh=mesh,
        in_specs=in_specs,
        out_specs=out_specs,
        check_vma=False,
    )
```

profile of v0, /device:TPU:3, one launch (start us, length us, event | category | flops | bytes accessed | tf_op | source)
XLA Modules:
  0.0 108.0 jit_solution(15815828864706634773)
XLA Ops:
  1.3 0.0 copy-start.1
  1.3 1.1 %copy-done.1 = f32[2,384,256]{2,1,0:T(8,128)S(1)} copy-done((f32[2,384,256]{2,1,0:T(8,128)S(1)}, f32[2,384,256]{2,1,0:T(8,128)}, u32[]{:S(2)}) %copy-start.1) | copy-done | bytes 786456
  2.4 0.0 copy-start.2
  2.4 21.7 %object_halo.1.ext = f32[2,640,512]{2,1,0:T(8,128)S(1)} custom-call(f32[2,384,256]{2,1,0:T(8,128)S(1)} %copy-done.1), custom_call_target="tpu_custom_call" | custom-call | tf_op jit(solution)/shard_map/object_halo/pallas_call | solution.py:340
  24.1 0.0 copy-start
  24.1 1.5 %copy-done = f32[2,640,512]{2,1,0:T(8,128)} copy-done((f32[2,640,512]{2,1,0:T(8,128)}, f32[2,640,512]{2,1,0:T(8,128)S(1)}, u32[]{:S(2)}) %copy-start) | copy-done | bytes 2621464
  25.6 0.0 copy-start.3
  25.6 1.0 copy-done.3
  26.7 0.0 copy-start.4
  26.7 1.0 copy-done.4
  27.7 0.0 copy-start.5
  27.7 1.0 copy-done.5
  28.7 0.0 copy-start.6
  28.7 1.0 copy-done.6
  29.8 0.0 copy-start.7
  29.8 1.0 copy-done.7
  30.8 0.0 copy-start.8
  30.8 1.0 copy-done.8
  31.9 0.0 copy-start.9
  31.9 0.7 copy-done.9
  32.5 0.0 copy-start.10
  32.5 0.7 copy-done.10
  33.2 0.0 copy-start.11
  33.2 0.7 copy-done.11
  33.8 9.8 %scan_terms.1 = (f32[3,640,512]{2,1,0:T(8,128)}, f32[3,32,8,256]{3,2,1,0:T(8,128)S(1)}) custom-call(s32[4]{0:T(128)S(1)} %bitcast.9, s32[4]{0:T(128)S(1)} %bitcast.10, s32[2]{0:T(128)S(1)} %bitcast.11, s32[1]{0:T(128)S(6)} %copy.15.count, f32[2,640,512]{2,1,0:T(8,128)} %copy-done, f32[2,256,256]{2,1,0:T(8,128)S(1)} %copy-done.3, ...), custom_call_target="tpu_custom_call" | custom-call | tf_op jit(solution)/shard_map/scan_terms/pallas_call | solution.py:351
  43.7 0.0 copy-done.2
  43.7 62.7 %fold.1 = (f32[2,384,256]{2,1,0:T(8,128)S(1)}, f32[2,32,8,256]{3,2,1,0:T(8,128)S(1)}) custom-call(f32[3,640,512]{2,1,0:T(8,128)} %get-tuple-element.6.refs_0_, f32[3,32,8,256]{3,2,1,0:T(8,128)S(1)} %get-tuple-element.7.refs_1_, f32[2,384,256]{2,1,0:T(8,128)S(1)} %copy-done.2, f32[2,32,8,256]{3,2,1,0:T(8,128)S(1)} %bitcast.6), custom_call_target="tpu_custom_call" | custom-call | tf_op jit(solution)/shard_map/fold/pallas_call | solution.py:383
  106.4 0.9 copy.16
  107.2 0.8 copy.17
Async XLA Ops:
  1.3 1.1 %copy-start.1 = (f32[2,384,256]{2,1,0:T(8,128)S(1)}, f32[2,384,256]{2,1,0:T(8,128)}, u32[]{:S(2)}) copy-start(f32[2,384,256]{2,1,0:T(8,128)} %refs_2_.1) | copy-start | bytes 2359300
  2.4 41.3 %copy-start.2 = (f32[2,384,256]{2,1,0:T(8,128)S(1)}, f32[2,384,256]{2,1,0:T(8,128)}, u32[]{:S(2)}) copy-start(f32[2,384,256]{2,1,0:T(8,128)} %refs_2_.1) | copy-start | bytes 2359300
  24.1 1.5 %copy-start = (f32[2,640,512]{2,1,0:T(8,128)}, f32[2,640,512]{2,1,0:T(8,128)S(1)}, u32[]{:S(2)}) copy-start(f32[2,640,512]{2,1,0:T(8,128)S(1)} %object_halo.1.ext) | copy-start | bytes 7864324
  25.6 1.0 copy-start.3
  26.7 1.0 copy-start.4
  27.7 1.0 copy-start.5
  28.7 1.0 copy-start.6
  29.8 1.0 copy-start.7
  30.8 1.0 copy-start.8
  31.9 0.7 copy-start.9
  32.5 0.7 copy-start.10
  33.2 0.7 copy-start.11
where the time goes:
time: 110 us; the launch traced here: 108 us
  Pallas kernels  94.2 us (86%)
  local copies, waits for them, and re-layouts  12.5 us (11%)
  between operations  1.32 us (1%)
    pallas_call x1, Pallas kernels, per_device(): pl.pallas_call(functools.partial(fold_kernel, sizes, rim, steps, 4), out_...  62.7 us
    pallas_call x1, Pallas kernels, per_device(): pl.pallas_call(functools.partial(halo_kernel, sizes, rim), out_shape=jax....  21.7 us
    unnamed x26, local copies, waits for them, and re-layouts  12.5 us
    pallas_call x1, Pallas kernels, per_device(): pl.pallas_call(work_kernel, out_shape=[jax.ShapeDtypeStruct((3,) + outer,...  9.82 us

commit v1 on v0

--- a/solution.py
+++ b/solution.py
@@ -16,7 +16,7 @@
 MESH = pl.DeviceIdType.MESH
 VMEM_BYTES = 48 * 1024 * 1024
 SUB = 8
-WAYS = [(-1, 0), (1, 0), (0, -1), (0, 1), (-1, -1), (-1, 1), (1, -1), (1, 1)]
+WAYS = [(-1, 0), (1, 0), (0, -1), (0, 1)]
 F32 = jnp.float32
 
 
@@ -58,14 +58,23 @@
     src = {-1: lambda n: (0, rim), 0: lambda n: (0, n), 1: lambda n: (n - rim, rim)}
     dst = {-1: lambda n: (rim + n, rim), 0: lambda n: (rim, n), 1: lambda n: (0, rim)}
 
-    def cut(ref, table, way):
-        r, c = table[way[0]](high), table[way[1]](wide)
-        return ref.at[:, pl.ds(*r), pl.ds(*c)]
+    def ends(way):
+        if way[0]:
+            inner = pl.ds(rim, wide)
+            return (
+                obj.at[:, pl.ds(*src[way[0]](high)), :],
+                ext.at[:, pl.ds(*dst[way[0]](high)), inner],
+            )
+        start, size = src[way[1]](wide)
+        return (
+            ext.at[:, :, pl.ds(start + rim, size)],
+            ext.at[:, :, pl.ds(*dst[way[1]](wide))],
+        )
 
     copies = [
         pltpu.make_async_remote_copy(
-            src_ref=cut(obj, src, way),
-            dst_ref=cut(ext, dst, way),
+            src_ref=ends(way)[0],
+            dst_ref=ends(way)[1],
             send_sem=send_sem.at[k],
             recv_sem=recv_sem.at[k],
             device_id=(at[0] + way[0], at[1] + way[1]),
@@ -73,21 +82,34 @@
         )
         for k, way in enumerate(WAYS)
     ]
-    for copy, way in zip(copies, WAYS):
+    both = list(zip(copies, WAYS))
+    for copy, way in both[:2]:
         pl.when(exists(at, way, sizes, 1))(copy.start)
     own = pltpu.make_async_copy(obj, ext.at[:, pl.ds(rim, high), pl.ds(rim, wide)], own_sem)
     own.start()
-    for way in WAYS:
+    for way in WAYS[:2]:
 
         @pl.when(jnp.logical_not(exists(at, way, sizes, -1)))
         def _(way=way):
-            (r, nr), (c, nc) = dst[way[0]](high), dst[way[1]](wide)
-            ext[:, r : r + nr, c : c + nc] = jnp.zeros((2, nr, nc), F32)
+            r, nr = dst[way[0]](high)
+            ext[:, r : r + nr, rim : rim + wide] = jnp.zeros((2, nr, wide), F32)
+
+    for way in WAYS[2:]:
+
+        @pl.when(jnp.logical_not(exists(at, way, sizes, -1)))
+        def _(way=way):
+            c, nc = dst[way[1]](wide)
+            ext[:, :, c : c + nc] = jnp.zeros((2, high + 2 * rim, nc), F32)
 
     own.wait()
-    for copy, way in zip(copies, WAYS):
+    for copy, way in both[:2]:
+        pl.when(exists(at, way, sizes, -1))(copy.wait_recv)
+    for copy, way in both[2:]:
+        pl.when(exists(at, way, sizes, 1))(copy.start)
+    for copy, way in both[2:]:
+        pl.when(exists(at, way, sizes, -1))(copy.wait_recv)
+    for copy, way in both:
         pl.when(exists(at, way, sizes, 1))(copy.wait_send)
-        pl.when(exists(at, way, sizes, -1))(copy.wait_recv)
 
 
 def split(x):
@@ -110,8 +132,13 @@
 
 
 def work_kernel(
-    rows, cols, picks, count, ext, probe, amps, m_hi, m_lo, n_hi, n_lo, grad, sums, obj, wave
+    rows, cols, picks, count, ext, probe, *rest
 ):
+    late, (grad, sums, obj, wave), held, sems = rest[:5], rest[5:9], rest[9:14], rest[14]
+    loads = [pltpu.make_async_copy(a, b, sems.at[k]) for k, (a, b) in enumerate(zip(late, held))]
+    for load in loads:
+        load.start()
+    amps, m_hi, m_lo, n_hi, n_lo = held
     width = probe.shape[1]
     slots = picks.shape[0]
     span = ext.shape[2]
@@ -127,6 +154,9 @@
         here = slice(s * width, (s + 1) * width)
         wave[:width, here] = pr * obj[s, 0] - pi * obj[s, 1]
         wave[width:, here] = pr * obj[s, 1] + pi * obj[s, 0]
+
+    for load in loads:
+        load.wait()
 
     def turn(x):
         return jnp.concatenate(
@@ -188,7 +218,9 @@
     grad, sums, obj, probe, obj_out, probe_out, acc, cen = refs[:8]
     bufs = refs[8 : 8 + len(WAYS)]
     stage_bufs = refs[8 + len(WAYS) : 8 + len(WAYS) + len(steps)]
-    send_sem, recv_sem, rs_send, rs_recv, ag_send, ag_recv = refs[8 + len(WAYS) + len(steps) :]
+    strips, send_sem, recv_sem, rs_send, rs_recv, ag_send, ag_recv = refs[
+        8 + len(WAYS) + len(steps) :
+    ]
     high, wide = obj.shape[1:]
     at = place(sizes)
 
@@ -206,10 +238,9 @@
     dst = {-1: lambda n: (n - rim, rim), 0: lambda n: (0, n), 1: lambda n: (0, rim)}
     copies = []
     for k, way in enumerate(WAYS):
-        r, c = src[way[0]](high), src[way[1]](wide)
         copies.append(
             pltpu.make_async_remote_copy(
-                src_ref=grad.at[:, pl.ds(*r), pl.ds(*c)],
+                src_ref=strips.at[k] if way[0] else grad.at[:, :, pl.ds(*src[way[1]](wide))],
                 dst_ref=bufs[k],
                 send_sem=send_sem.at[k],
                 recv_sem=recv_sem.at[k],
@@ -218,8 +249,29 @@
             )
         )
 
-    def begin_halo():
-        for copy, way in zip(copies, WAYS):
+    both = list(zip(copies, WAYS))
+
+    def begin_cols():
+        for copy, way in both[2:]:
+            pl.when(exists(at, way, sizes, 1))(copy.start)
+
+    def begin_rows():
+        cen[...] = grad[:, rim : rim + high, rim : rim + wide]
+        for k, way in enumerate(WAYS[:2]):
+            r, nr = src[way[0]](high)
+            strips[k] = grad[:, r : r + nr, rim : rim + wide]
+        for j, (copy, side) in enumerate(both[2:], 2):
+
+            @pl.when(exists(at, side, sizes, -1))
+            def _(j=j, copy=copy, side=side):
+                copy.wait_recv()
+                c, nc = dst[side[1]](wide)
+                cen[:, :, c : c + nc] += bufs[j][:, rim : rim + high, :]
+                for k, way in enumerate(WAYS[:2]):
+                    r, nr = src[way[0]](high)
+                    strips[k, :, :, c : c + nc] += bufs[j][:, r : r + nr, :]
+
+        for copy, way in both[:2]:
             pl.when(exists(at, way, sizes, 1))(copy.start)
 
     acc[...] = sums[...]
@@ -247,7 +299,9 @@
             moved.append(copy)
             sem += 1
         if i == 0:
-            begin_halo()
+            begin_cols()
+        if i == min(1, len(steps) - 1):
+            begin_rows()
         digit = peer(step, 1)[1]
         for copy in moved:
             copy.wait_recv()
@@ -273,14 +327,13 @@
         probe_out[p, pl.ds(off, part)] = probe[p, pl.ds(off, part)] + acc[p, pl.ds(off, part)] / reg
 
     def finish_object():
-        cen[...] = grad[:, rim : rim + high, rim : rim + wide]
-        for k, (copy, way) in enumerate(zip(copies, WAYS)):
+        for k, (copy, way) in enumerate(both[:2]):
 
             @pl.when(exists(at, way, sizes, -1))
             def _(k=k, copy=copy, way=way):
                 copy.wait_recv()
-                (r, nr), (c, nc) = dst[way[0]](high), dst[way[1]](wide)
-                cen[:, r : r + nr, c : c + nc] += bufs[k][...]
+                r, nr = dst[way[0]](high)
+                cen[:, r : r + nr, :] += bufs[k][...]
 
         light = cen[2] + OBJECT_REG
         for p in range(2):
@@ -354,11 +407,16 @@
             jax.ShapeDtypeStruct((3,) + outer, F32),
             jax.ShapeDtypeStruct((3, width // SUB, SUB, width), F32),
         ],
-        in_specs=[smem] * 4 + [vmem] * 7,
+        in_specs=[smem] * 4 + [vmem] * 2 + [pl.BlockSpec(memory_space=pl.ANY)] * 5,
         out_specs=[vmem, vmem],
         scratch_shapes=[
             pltpu.VMEM((slots, 2, width, width), F32),
             pltpu.VMEM((2 * width, slots * width), F32),
+            pltpu.VMEM(amplitudes.shape[2:], jnp.bfloat16),
+        ]
+        + [pltpu.VMEM((2 * width, 2 * width), jnp.bfloat16)] * 4
+        + [
+            dma((5,)),
         ],
         compiler_params=pltpu.CompilerParams(vmem_limit_bytes=VMEM_BYTES),
         name="scan_terms",
@@ -379,7 +437,6 @@
         steps.append((axis, stride, p, size, scatter))
         size = size // p if scatter else size
     sems = sum(step[2] - 1 for step in steps)
-    lengths = {-1: lambda n: rim, 0: lambda n: n, 1: lambda n: rim}
     object_next, probe_next = pl.pallas_call(
         functools.partial(fold_kernel, sizes, rim, steps, 4),
         out_shape=[
@@ -392,11 +449,12 @@
             pltpu.VMEM((3, width // SUB, SUB, width), F32),
             pltpu.VMEM((3, high, wide), F32),
         ]
-        + [pltpu.VMEM((3, lengths[r](high), lengths[c](wide)), F32) for r, c in WAYS]
+        + [pltpu.VMEM((3, rim, wide) if r else (3, outer[0], rim), F32) for r, c in WAYS]
         + [
             pltpu.VMEM((p, 3, size // p if scatter else size, SUB, width), F32)
             for _, _, p, size, scatter in steps
         ]
+        + [pltpu.VMEM((2, 3, rim, wide), F32)]
         + [dma((len(WAYS),)), dma((len(WAYS),))]
         + [dma((sems,))] * 4,
         compiler_params=pltpu.CompilerParams(

time: 110 us -> 104 us (0.945)
  the two profiles are of different devices: /device:TPU:3 before, /device:TPU:1 now
where the time goes in v1:
time: 104 us; the launch traced here: 103 us
  Pallas kernels  89.5 us (86%)
  local copies, waits for them, and re-layouts  12.5 us (12%)
  between operations  1.34 us (1%)
    pallas_call x1, Pallas kernels, per_device(): pl.pallas_call(functools.partial(fold_kernel, sizes, rim, steps, 4), out_...  59.4 us
    pallas_call x1, Pallas kernels, per_device(): pl.pallas_call(functools.partial(halo_kernel, sizes, rim), out_shape=jax....  20 us
    unnamed x26, local copies, waits for them, and re-layouts  12.5 us
    pallas_call x1, Pallas kernels, per_device(): pl.pallas_call(work_kernel, out_shape=[jax.ShapeDtypeStruct((3,) + outer,...  10.1 us

profile of v1, /device:TPU:1, one launch (start us, length us, event | category | flops | bytes accessed | tf_op | source)
XLA Modules:
  0.0 103.4 jit_solution(1981509844885617780)
XLA Ops:
  1.3 0.0 copy-start.1
  1.3 1.1 %copy-done.1 = f32[2,384,256]{2,1,0:T(8,128)S(1)} copy-done((f32[2,384,256]{2,1,0:T(8,128)S(1)}, f32[2,384,256]{2,1,0:T(8,128)}, u32[]{:S(2)}) %copy-start.1) | copy-done | bytes 786456
  2.4 0.0 copy-start.2
  2.4 20.0 %object_halo.1.ext = f32[2,640,512]{2,1,0:T(8,128)S(1)} custom-call(f32[2,384,256]{2,1,0:T(8,128)S(1)} %copy-done.1), custom_call_target="tpu_custom_call" | custom-call | tf_op jit(solution)/shard_map/object_halo/pallas_call | solution.py:393
  22.4 0.0 copy-start
  22.4 1.5 %copy-done = f32[2,640,512]{2,1,0:T(8,128)} copy-done((f32[2,640,512]{2,1,0:T(8,128)}, f32[2,640,512]{2,1,0:T(8,128)S(1)}, u32[]{:S(2)}) %copy-start) | copy-done | bytes 2621464
  24.0 0.0 copy-start.3
  24.0 1.0 %copy-done.3 = f32[2,256,256]{2,1,0:T(8,128)S(1)} copy-done((f32[2,256,256]{2,1,0:T(8,128)S(1)}, f32[2,256,256]{2,1,0:T(8,128)}, u32[]{:S(2)}) %copy-start.3) | copy-done | bytes 524312
  25.0 0.0 copy-start.4
  25.0 1.0 %copy-done.4 = bf16[1,1,4,256,256]{4,3,2,1,0:T(8,128)(2,1)S(1)} copy-done((bf16[1,1,4,256,256]{4,3,2,1,0:T(8,128)(2,1)S(1)}, bf16[1,1,4,256,256]{4,3,2,1,0:T(8,128)(2,1)}, u32[]{:S(2)}) %copy-start.4) | copy-done | bytes 524312
  26.0 0.0 copy-start.5
  26.0 1.0 %copy-done.5 = bf16[512,512]{1,0:T(8,128)(2,1)S(1)} copy-done((bf16[512,512]{1,0:T(8,128)(2,1)S(1)}, bf16[512,512]{1,0:T(8,128)(2,1)}, u32[]{:S(2)}) %copy-start.5) | copy-done | bytes 524312
  27.1 0.0 copy-start.6
  27.1 1.0 %copy-done.6 = bf16[512,512]{1,0:T(8,128)(2,1)S(1)} copy-done((bf16[512,512]{1,0:T(8,128)(2,1)S(1)}, bf16[512,512]{1,0:T(8,128)(2,1)}, u32[]{:S(2)}) %copy-start.6) | copy-done | bytes 524312
  28.1 0.0 copy-start.7
  28.1 1.0 %copy-done.7 = bf16[512,512]{1,0:T(8,128)(2,1)S(1)} copy-done((bf16[512,512]{1,0:T(8,128)(2,1)S(1)}, bf16[512,512]{1,0:T(8,128)(2,1)}, u32[]{:S(2)}) %copy-start.7) | copy-done | bytes 524312
  29.2 0.0 copy-start.8
  29.2 1.0 %copy-done.8 = bf16[512,512]{1,0:T(8,128)(2,1)S(1)} copy-done((bf16[512,512]{1,0:T(8,128)(2,1)S(1)}, bf16[512,512]{1,0:T(8,128)(2,1)}, u32[]{:S(2)}) %copy-start.8) | copy-done | bytes 524312
  30.2 0.0 copy-start.9
  30.2 0.7 copy-done.9
  30.9 0.0 copy-start.10
  30.9 0.7 copy-done.10
  31.5 0.0 copy-start.11
  31.5 0.7 copy-done.11
  32.2 10.1 %scan_terms.1 = (f32[3,640,512]{2,1,0:T(8,128)}, f32[3,32,8,256]{3,2,1,0:T(8,128)S(1)}) custom-call(s32[4]{0:T(128)S(1)} %bitcast.9, s32[4]{0:T(128)S(1)} %bitcast.10, s32[2]{0:T(128)S(1)} %bitcast.11, s32[1]{0:T(128)S(6)} %copy.15.count, f32[2,640,512]{2,1,0:T(8,128)} %copy-done, f32[2,256,256]{2,1,0:T(8,128)S(1)} %copy-done.3, ...), custom_call_target="tpu_custom_call" | custom-call | tf_op jit(solution)/shard_map/scan_terms/pallas_call | solution.py:404
  42.3 0.0 copy-done.2
  42.3 59.4 %fold.1 = (f32[2,384,256]{2,1,0:T(8,128)S(1)}, f32[2,32,8,256]{3,2,1,0:T(8,128)S(1)}) custom-call(f32[3,640,512]{2,1,0:T(8,128)} %get-tuple-element.6.refs_0_, f32[3,32,8,256]{3,2,1,0:T(8,128)S(1)} %get-tuple-element.7.refs_1_, f32[2,384,256]{2,1,0:T(8,128)S(1)} %copy-done.2, f32[2,32,8,256]{3,2,1,0:T(8,128)S(1)} %bitcast.6), custom_call_target="tpu_custom_call" | custom-call | tf_op jit(solution)/shard_map/fold/pallas_call | solution.py:440
  101.7 0.9 copy.16
  102.6 0.8 copy.17
Async XLA Ops:
  1.3 1.1 %copy-start.1 = (f32[2,384,256]{2,1,0:T(8,128)S(1)}, f32[2,384,256]{2,1,0:T(8,128)}, u32[]{:S(2)}) copy-start(f32[2,384,256]{2,1,0:T(8,128)} %refs_2_.1) | copy-start | bytes 2359300
  2.4 39.9 %copy-start.2 = (f32[2,384,256]{2,1,0:T(8,128)S(1)}, f32[2,384,256]{2,1,0:T(8,128)}, u32[]{:S(2)}) copy-start(f32[2,384,256]{2,1,0:T(8,128)} %refs_2_.1) | copy-start | bytes 2359300
  22.4 1.5 %copy-start = (f32[2,640,512]{2,1,0:T(8,128)}, f32[2,640,512]{2,1,0:T(8,128)S(1)}, u32[]{:S(2)}) copy-start(f32[2,640,512]{2,1,0:T(8,128)S(1)} %object_halo.1.ext) | copy-start | bytes 7864324
  24.0 1.0 %copy-start.3 = (f32[2,256,256]{2,1,0:T(8,128)S(1)}, f32[2,256,256]{2,1,0:T(8,128)}, u32[]{:S(2)}) copy-start(f32[2,256,256]{2,1,0:T(8,128)} %probe.1) | copy-start | bytes 1572868
  25.0 1.0 %copy-start.4 = (bf16[1,1,4,256,256]{4,3,2,1,0:T(8,128)(2,1)S(1)}, bf16[1,1,4,256,256]{4,3,2,1,0:T(8,128)(2,1)}, u32[]{:S(2)}) copy-start(bf16[1,1,4,256,256]{4,3,2,1,0:T(8,128)(2,1)} %param.13) | copy-start | bytes 1572868
  26.0 1.0 %copy-start.5 = (bf16[512,512]{1,0:T(8,128)(2,1)S(1)}, bf16[512,512]{1,0:T(8,128)(2,1)}, u32[]{:S(2)}) copy-start(bf16[512,512]{1,0:T(8,128)(2,1)} %constant.11.clone.rest_4_) | copy-start | bytes 1572868
  27.1 1.0 %copy-start.6 = (bf16[512,512]{1,0:T(8,128)(2,1)S(1)}, bf16[512,512]{1,0:T(8,128)(2,1)}, u32[]{:S(2)}) copy-start(bf16[512,512]{1,0:T(8,128)(2,1)} %constant.10.clone.rest_3_) | copy-start | bytes 1572868
  28.1 1.0 %copy-start.7 = (bf16[512,512]{1,0:T(8,128)(2,1)S(1)}, bf16[512,512]{1,0:T(8,128)(2,1)}, u32[]{:S(2)}) copy-start(bf16[512,512]{1,0:T(8,128)(2,1)} %constant.9.clone.rest_2_) | copy-start | bytes 1572868
  29.2 1.0 %copy-start.8 = (bf16[512,512]{1,0:T(8,128)(2,1)S(1)}, bf16[512,512]{1,0:T(8,128)(2,1)}, u32[]{:S(2)}) copy-start(bf16[512,512]{1,0:T(8,128)(2,1)} %constant.8.clone.rest_1_) | copy-start | bytes 1572868
  30.2 0.7 copy-start.9
  30.9 0.7 copy-start.10
  31.5 0.7 copy-start.11

commit v2 on v1

--- a/solution.py
+++ b/solution.py
@@ -134,11 +134,12 @@
 def work_kernel(
     rows, cols, picks, count, ext, probe, *rest
 ):
-    late, (grad, sums, obj, wave), held, sems = rest[:5], rest[5:9], rest[9:14], rest[14]
+    late, (grad, sums, obj, wave), held, sems = rest[:2], rest[2:6], rest[6:8], rest[12]
     loads = [pltpu.make_async_copy(a, b, sems.at[k]) for k, (a, b) in enumerate(zip(late, held))]
     for load in loads:
         load.start()
-    amps, m_hi, m_lo, n_hi, n_lo = held
+    amps, half = held
+    m_hi, m_lo, n_hi, n_lo = rest[8:12]
     width = probe.shape[1]
     slots = picks.shape[0]
     span = ext.shape[2]
@@ -157,6 +158,12 @@
 
     for load in loads:
         load.wait()
+    one, two = slice(0, width), slice(width, 2 * width)
+    for part, m, n in ((0, m_hi, n_hi), (1, m_lo, n_lo)):
+        cos, sin = half[part, one], half[part, two]
+        for t, up, down in ((m, -sin, sin), (n, sin, -sin)):
+            t[one, one], t[one, two] = cos, up
+            t[two, one], t[two, two] = down, cos
 
     def turn(x):
         return jnp.concatenate(
@@ -300,7 +307,7 @@
             sem += 1
         if i == 0:
             begin_cols()
-        if i == min(1, len(steps) - 1):
+        if i == min(2, len(steps) - 1):
             begin_rows()
         digit = peer(step, 1)[1]
         for copy in moved:
@@ -357,10 +364,11 @@
             copy.start()
             moved.append(copy)
             sem += 1
+        if n == max(0, len(undo) - 3):
+            finish_object()
         for copy in moved:
             copy.wait_recv()
         pending += moved
-    finish_object()
     for copy in pending:
         copy.wait_send()
     for copy, way in zip(copies, WAYS):
@@ -371,12 +379,9 @@
     grid = np.arange(width)
     angle = (grid[:, None] * grid[None, :] % width) * (2.0 * math.pi / width)
     cos, sin = np.cos(angle) / math.sqrt(width), -np.sin(angle) / math.sqrt(width)
-    out = []
-    for full in (np.block([[cos, -sin], [sin, cos]]), np.block([[cos, sin], [-sin, cos]])):
-        full = full.astype(np.float32)
-        hi = full.astype(ml_dtypes.bfloat16)
-        out += [hi, (full - hi.astype(np.float32)).astype(ml_dtypes.bfloat16)]
-    return out
+    full = np.concatenate([cos, sin], axis=0).astype(np.float32)
+    hi = full.astype(ml_dtypes.bfloat16)
+    return np.stack([hi, (full - hi.astype(np.float32)).astype(ml_dtypes.bfloat16)])
 
 
 def per_device(
@@ -407,16 +412,17 @@
             jax.ShapeDtypeStruct((3,) + outer, F32),
             jax.ShapeDtypeStruct((3, width // SUB, SUB, width), F32),
         ],
-        in_specs=[smem] * 4 + [vmem] * 2 + [pl.BlockSpec(memory_space=pl.ANY)] * 5,
+        in_specs=[smem] * 4 + [vmem] * 2 + [pl.BlockSpec(memory_space=pl.ANY)] * 2,
         out_specs=[vmem, vmem],
         scratch_shapes=[
             pltpu.VMEM((slots, 2, width, width), F32),
             pltpu.VMEM((2 * width, slots * width), F32),
             pltpu.VMEM(amplitudes.shape[2:], jnp.bfloat16),
+            pltpu.VMEM((2, 2 * width, width), jnp.bfloat16),
         ]
         + [pltpu.VMEM((2 * width, 2 * width), jnp.bfloat16)] * 4
         + [
-            dma((5,)),
+            dma((2,)),
         ],
         compiler_params=pltpu.CompilerParams(vmem_limit_bytes=VMEM_BYTES),
         name="scan_terms",
@@ -428,7 +434,7 @@
         ext,
         probe_field,
         amplitudes[0, 0],
-        *tables(width),
+        tables(width),
     )
     size = width // SUB
     steps = []

time: 104 us -> 97.1 us (0.934)
  the two profiles are of different devices: /device:TPU:1 before, /device:TPU:3 now
where the time goes in v2:
time: 97.1 us; the launch traced here: 96.8 us
  Pallas kernels  87.5 us (90%)
  local copies, waits for them, and re-layouts  7.89 us (8%)
  between operations  1.33 us (1%)
    pallas_call x1, Pallas kernels, per_device(): pl.pallas_call(functools.partial(fold_kernel, sizes, rim, steps, 4), out_...  66.8 us
    pallas_call x1, Pallas kernels, per_device(): pl.pallas_call(functools.partial(halo_kernel, sizes, rim), out_shape=jax....  11.9 us
    pallas_call x1, Pallas kernels, per_device(): pl.pallas_call(work_kernel, out_shape=[jax.ShapeDtypeStruct((3,) + outer,...  8.83 us
    unnamed x18, local copies, waits for them, and re-layouts  7.89 us

profile of v2, /device:TPU:3, one launch (start us, length us, event | category | flops | bytes accessed | tf_op | source)
XLA Modules:
  0.0 96.8 jit_solution(4155674900760500432)
XLA Ops:
  1.3 0.0 copy-start
  1.3 1.1 %copy-done = f32[2,384,256]{2,1,0:T(8,128)S(1)} copy-done((f32[2,384,256]{2,1,0:T(8,128)S(1)}, f32[2,384,256]{2,1,0:T(8,128)}, u32[]{:S(2)}) %copy-start) | copy-done | bytes 786456
  2.4 0.0 copy-start.2
  2.4 11.9 %object_halo.1.ext = f32[2,640,512]{2,1,0:T(8,128)S(1)} custom-call(f32[2,384,256]{2,1,0:T(8,128)S(1)} %copy-done), custom_call_target="tpu_custom_call" | custom-call | tf_op jit(solution)/shard_map/object_halo/pallas_call | solution.py:398
  14.4 0.0 copy-start.1
  14.4 1.0 %copy-done.1 = f32[2,256,256]{2,1,0:T(8,128)S(1)} copy-done((f32[2,256,256]{2,1,0:T(8,128)S(1)}, f32[2,256,256]{2,1,0:T(8,128)}, u32[]{:S(2)}) %copy-start.1) | copy-done | bytes 524312
  15.4 0.0 copy-start.3
  15.4 1.0 %copy-done.3 = bf16[1,1,4,256,256]{4,3,2,1,0:T(8,128)(2,1)S(1)} copy-done((bf16[1,1,4,256,256]{4,3,2,1,0:T(8,128)(2,1)S(1)}, bf16[1,1,4,256,256]{4,3,2,1,0:T(8,128)(2,1)}, u32[]{:S(2)}) %copy-start.3) | copy-done | bytes 524312
  16.4 0.0 copy-start.4
  16.4 1.0 %copy-done.4 = bf16[2,512,256]{2,1,0:T(8,128)(2,1)S(1)} copy-done((bf16[2,512,256]{2,1,0:T(8,128)(2,1)S(1)}, bf16[2,512,256]{2,1,0:T(8,128)(2,1)}, u32[]{:S(2)}) %copy-start.4) | copy-done | bytes 524312
  17.5 0.0 copy-start.5
  17.5 0.7 copy-done.5
  18.1 0.0 copy-start.6
  18.1 0.7 copy-done.6
  18.8 0.0 copy-start.7
  18.8 0.7 copy-done.7
  19.5 8.8 %scan_terms.1 = (f32[3,640,512]{2,1,0:T(8,128)}, f32[3,32,8,256]{3,2,1,0:T(8,128)S(1)}) custom-call(s32[4]{0:T(128)S(1)} %bitcast.9, s32[4]{0:T(128)S(1)} %bitcast.10, s32[2]{0:T(128)S(1)} %bitcast.11, s32[1]{0:T(128)S(6)} %copy.12.count, f32[2,640,512]{2,1,0:T(8,128)S(1)} %object_halo.1.ext, f32[2,256,256]{2,1,0:T(8,128)S(1)} %copy-done.1, ...), custom_call_target="tpu_custom_call" | custom-call | tf_op jit(solution)/shard_map/scan_terms/pallas_call | solution.py:409
  28.3 0.0 copy-done.2
  28.3 66.8 %fold.1 = (f32[2,384,256]{2,1,0:T(8,128)S(1)}, f32[2,32,8,256]{3,2,1,0:T(8,128)S(1)}) custom-call(f32[3,640,512]{2,1,0:T(8,128)} %get-tuple-element.6.refs_0_, f32[3,32,8,256]{3,2,1,0:T(8,128)S(1)} %get-tuple-element.7.refs_1_, f32[2,384,256]{2,1,0:T(8,128)S(1)} %copy-done, f32[2,32,8,256]{3,2,1,0:T(8,128)S(1)} %bitcast.6), custom_call_target="tpu_custom_call" | custom-call | tf_op jit(solution)/shard_map/fold/pallas_call | solution.py:446
  95.1 0.9 copy.13
  96.0 0.8 copy.14
Async XLA Ops:
  1.3 1.1 %copy-start = (f32[2,384,256]{2,1,0:T(8,128)S(1)}, f32[2,384,256]{2,1,0:T(8,128)}, u32[]{:S(2)}) copy-start(f32[2,384,256]{2,1,0:T(8,128)} %refs_2_.1) | copy-start | bytes 2359300
  2.4 25.9 %copy-start.2 = (f32[2,256,256]{2,1,0:T(8,128)S(1)}, f32[2,256,256]{2,1,0:T(8,128)}, u32[]{:S(2)}) copy-start(f32[2,256,256]{2,1,0:T(8,128)} %probe.1) | copy-start | bytes 1572868
  14.4 1.0 %copy-start.1 = (f32[2,256,256]{2,1,0:T(8,128)S(1)}, f32[2,256,256]{2,1,0:T(8,128)}, u32[]{:S(2)}) copy-start(f32[2,256,256]{2,1,0:T(8,128)} %probe.1) | copy-start | bytes 1572868
  15.4 1.0 %copy-start.3 = (bf16[1,1,4,256,256]{4,3,2,1,0:T(8,128)(2,1)S(1)}, bf16[1,1,4,256,256]{4,3,2,1,0:T(8,128)(2,1)}, u32[]{:S(2)}) copy-start(bf16[1,1,4,256,256]{4,3,2,1,0:T(8,128)(2,1)} %param.10) | copy-start | bytes 1572868
  16.4 1.0 %copy-start.4 = (bf16[2,512,256]{2,1,0:T(8,128)(2,1)S(1)}, bf16[2,512,256]{2,1,0:T(8,128)(2,1)}, u32[]{:S(2)}) copy-start(bf16[2,512,256]{2,1,0:T(8,128)(2,1)} %constant.2.clone.rest_1_) | copy-start | bytes 1572868
  17.5 0.7 copy-start.5
  18.1 0.7 copy-start.6
  18.8 0.7 copy-start.7

commit v3 on v2

--- a/solution.py
+++ b/solution.py
@@ -71,19 +71,29 @@
             ext.at[:, :, pl.ds(*dst[way[1]](wide))],
         )
 
-    copies = [
-        pltpu.make_async_remote_copy(
-            src_ref=ends(way)[0],
-            dst_ref=ends(way)[1],
+    def send(ref, target, way, k):
+        return pltpu.make_async_remote_copy(
+            src_ref=ref,
+            dst_ref=target,
             send_sem=send_sem.at[k],
             recv_sem=recv_sem.at[k],
             device_id=(at[0] + way[0], at[1] + way[1]),
             device_id_type=MESH,
         )
-        for k, way in enumerate(WAYS)
-    ]
-    both = list(zip(copies, WAYS))
-    for copy, way in both[:2]:
+
+    both = [(send(*ends(way), way, k), way) for k, way in enumerate(WAYS[:2])]
+    corners = []
+    for way in WAYS[2:]:
+        near, far = pl.ds(*src[way[1]](wide)), pl.ds(*dst[way[1]](wide))
+        middle = send(obj.at[:, :, near], ext.at[:, pl.ds(rim, high), far], way, len(both))
+        both.append((middle, way))
+    for way in WAYS[2:]:
+        whole, target = ends(way)
+        for top in (0, rim + high):
+            piece = pl.ds(top, rim)
+            k = len(both) + len(corners)
+            corners.append((send(whole.at[:, piece, :], target.at[:, piece, :], way, k), way))
+    for copy, way in both:
         pl.when(exists(at, way, sizes, 1))(copy.start)
     own = pltpu.make_async_copy(obj, ext.at[:, pl.ds(rim, high), pl.ds(rim, wide)], own_sem)
     own.start()
@@ -104,11 +114,11 @@
     own.wait()
     for copy, way in both[:2]:
         pl.when(exists(at, way, sizes, -1))(copy.wait_recv)
-    for copy, way in both[2:]:
+    for copy, way in corners:
         pl.when(exists(at, way, sizes, 1))(copy.start)
-    for copy, way in both[2:]:
+    for copy, way in both[2:] + corners:
         pl.when(exists(at, way, sizes, -1))(copy.wait_recv)
-    for copy, way in both:
+    for copy, way in both + corners:
         pl.when(exists(at, way, sizes, 1))(copy.wait_send)
 
 
@@ -400,7 +410,7 @@
         out_shape=jax.ShapeDtypeStruct((2,) + outer, F32),
         in_specs=[vmem],
         out_specs=vmem,
-        scratch_shapes=[dma((len(WAYS),)), dma((len(WAYS),)), dma],
+        scratch_shapes=[dma((2 * len(WAYS),)), dma((2 * len(WAYS),)), dma],
         compiler_params=pltpu.CompilerParams(
             collective_id=0, has_side_effects=True, vmem_limit_bytes=VMEM_BYTES
         ),

time: 97.1 us -> 93 us (0.958)
  Pallas kernels: 87.5 us -> 83.4 us
    pallas_call x1, Pallas kernels: 66.8 us -> 62.6 us  [per_device(): pl.pallas_call(functools.partial(fold_kernel, sizes, rim, steps, 4), out_...]
where the time goes in v3:
time: 93 us; the launch traced here: 92.6 us
  Pallas kernels  83.4 us (90%)
  local copies, waits for them, and re-layouts  7.89 us (8%)
  between operations  1.33 us (1%)
    pallas_call x1, Pallas kernels, per_device(): pl.pallas_call(functools.partial(fold_kernel, sizes, rim, steps, 4), out_...  62.6 us
    pallas_call x1, Pallas kernels, per_device(): pl.pallas_call(functools.partial(halo_kernel, sizes, rim), out_shape=jax....  12 us
    pallas_call x1, Pallas kernels, per_device(): pl.pallas_call(work_kernel, out_shape=[jax.ShapeDtypeStruct((3,) + outer,...  8.83 us
    unnamed x18, local copies, waits for them, and re-layouts  7.89 us

profile of v3, /device:TPU:3, one launch (start us, length us, event | category | flops | bytes accessed | tf_op | source)
XLA Modules:
  0.0 92.6 jit_solution(2510456612032418891)
XLA Ops:
  1.3 0.0 copy-start
  1.3 1.1 %copy-done = f32[2,384,256]{2,1,0:T(8,128)S(1)} copy-done((f32[2,384,256]{2,1,0:T(8,128)S(1)}, f32[2,384,256]{2,1,0:T(8,128)}, u32[]{:S(2)}) %copy-start) | copy-done | bytes 786456
  2.4 0.0 copy-start.2
  2.4 12.0 %object_halo.1.ext = f32[2,640,512]{2,1,0:T(8,128)S(1)} custom-call(f32[2,384,256]{2,1,0:T(8,128)S(1)} %copy-done), custom_call_target="tpu_custom_call" | custom-call | tf_op jit(solution)/shard_map/object_halo/pallas_call | solution.py:408
  14.4 0.0 copy-start.1
  14.4 1.0 %copy-done.1 = f32[2,256,256]{2,1,0:T(8,128)S(1)} copy-done((f32[2,256,256]{2,1,0:T(8,128)S(1)}, f32[2,256,256]{2,1,0:T(8,128)}, u32[]{:S(2)}) %copy-start.1) | copy-done | bytes 524312
  15.5 0.0 copy-start.3
  15.5 1.0 %copy-done.3 = bf16[1,1,4,256,256]{4,3,2,1,0:T(8,128)(2,1)S(1)} copy-done((bf16[1,1,4,256,256]{4,3,2,1,0:T(8,128)(2,1)S(1)}, bf16[1,1,4,256,256]{4,3,2,1,0:T(8,128)(2,1)}, u32[]{:S(2)}) %copy-start.3) | copy-done | bytes 524312
  16.5 0.0 copy-start.4
  16.5 1.0 %copy-done.4 = bf16[2,512,256]{2,1,0:T(8,128)(2,1)S(1)} copy-done((bf16[2,512,256]{2,1,0:T(8,128)(2,1)S(1)}, bf16[2,512,256]{2,1,0:T(8,128)(2,1)}, u32[]{:S(2)}) %copy-start.4) | copy-done | bytes 524312
  17.6 0.0 copy-start.5
  17.6 0.7 copy-done.5
  18.2 0.0 copy-start.6
  18.2 0.7 copy-done.6
  18.9 0.0 copy-start.7
  18.9 0.7 copy-done.7
  19.5 8.8 %scan_terms.1 = (f32[3,640,512]{2,1,0:T(8,128)}, f32[3,32,8,256]{3,2,1,0:T(8,128)S(1)}) custom-call(s32[4]{0:T(128)S(1)} %bitcast.9, s32[4]{0:T(128)S(1)} %bitcast.10, s32[2]{0:T(128)S(1)} %bitcast.11, s32[1]{0:T(128)S(6)} %copy.12.count, f32[2,640,512]{2,1,0:T(8,128)S(1)} %object_halo.1.ext, f32[2,256,256]{2,1,0:T(8,128)S(1)} %copy-done.1, ...), custom_call_target="tpu_custom_call" | custom-call | tf_op jit(solution)/shard_map/scan_terms/pallas_call | solution.py:419
  28.4 0.0 copy-done.2
  28.4 62.6 %fold.1 = (f32[2,384,256]{2,1,0:T(8,128)S(1)}, f32[2,32,8,256]{3,2,1,0:T(8,128)S(1)}) custom-call(f32[3,640,512]{2,1,0:T(8,128)} %get-tuple-element.6.refs_0_, f32[3,32,8,256]{3,2,1,0:T(8,128)S(1)} %get-tuple-element.7.refs_1_, f32[2,384,256]{2,1,0:T(8,128)S(1)} %copy-done, f32[2,32,8,256]{3,2,1,0:T(8,128)S(1)} %bitcast.6), custom_call_target="tpu_custom_call" | custom-call | tf_op jit(solution)/shard_map/fold/pallas_call | solution.py:456
  90.9 0.9 copy.13
  91.8 0.8 copy.14
Async XLA Ops:
  1.3 1.1 %copy-start = (f32[2,384,256]{2,1,0:T(8,128)S(1)}, f32[2,384,256]{2,1,0:T(8,128)}, u32[]{:S(2)}) copy-start(f32[2,384,256]{2,1,0:T(8,128)} %refs_2_.1) | copy-start | bytes 2359300
  2.4 26.0 %copy-start.2 = (f32[2,256,256]{2,1,0:T(8,128)S(1)}, f32[2,256,256]{2,1,0:T(8,128)}, u32[]{:S(2)}) copy-start(f32[2,256,256]{2,1,0:T(8,128)} %probe.1) | copy-start | bytes 1572868
  14.4 1.0 %copy-start.1 = (f32[2,256,256]{2,1,0:T(8,128)S(1)}, f32[2,256,256]{2,1,0:T(8,128)}, u32[]{:S(2)}) copy-start(f32[2,256,256]{2,1,0:T(8,128)} %probe.1) | copy-start | bytes 1572868
  15.5 1.0 %copy-start.3 = (bf16[1,1,4,256,256]{4,3,2,1,0:T(8,128)(2,1)S(1)}, bf16[1,1,4,256,256]{4,3,2,1,0:T(8,128)(2,1)}, u32[]{:S(2)}) copy-start(bf16[1,1,4,256,256]{4,3,2,1,0:T(8,128)(2,1)} %param.10) | copy-start | bytes 1572868
  16.5 1.0 %copy-start.4 = (bf16[2,512,256]{2,1,0:T(8,128)(2,1)S(1)}, bf16[2,512,256]{2,1,0:T(8,128)(2,1)}, u32[]{:S(2)}) copy-start(bf16[2,512,256]{2,1,0:T(8,128)(2,1)} %constant.2.clone.rest_1_) | copy-start | bytes 1572868
  17.6 0.7 copy-start.5
  18.2 0.7 copy-start.6
  18.9 0.7 copy-start.7
